TPU v7x, 32 devices: a whole 2x2x4 slice. The times are simulated.
32 devices in a mesh: blk: 8 (over y, x, core), exp: 4 (over z).
Axes of the slice: x: 2, y: 2, z: 4, core: 2. Of those that a mesh axis runs over, the one named last changes fastest.
Arguments:
- residual_deposit_sequence: bfloat16 [4, 1024, 1536], P('exp', 'blk'), may hold values from -60 to 60
- premix_rescaler: float32 [1536], replicated, may hold values from 0.25 to 1.75
- asking_projector: bfloat16 [1536, 1536], P(None, 'exp'), may hold values from -0.15625 to 0.15625
- lookup_projector: bfloat16 [1536, 512], P(None, 'exp'), may hold values from -0.15625 to 0.15625
- content_projector: bfloat16 [1536, 512], P(None, 'exp'), may hold values from -0.15625 to 0.15625
- final_projector: bfloat16 [1536, 1536], P('exp'), may hold values from -0.15625 to 0.15625
- logit_multipliers: float32 [12], replicated, may hold values from 1.5 to 6
- premixture_rescaler: float32 [1536], replicated, may hold values from 0.25 to 1.75
- specialist_switch_tensor: bfloat16 [8, 1536, 384], P('exp'), may hold values from -0.15625 to 0.15625
- specialist_widen_tensor: bfloat16 [8, 1536, 384], P('exp'), may hold values from -0.15625 to 0.15625
- specialist_shrink_tensor: bfloat16 [8, 384, 1536], P('exp'), may hold values from -0.3125 to 0.3125
- picked_specialist_labels: int32 [4, 1024, 2], P(None, 'blk'), may hold values from 0 to 7, all different within a row; in each aligned block of 128 rows (0 to 127, 128 to 255, ..., all dimensions but the last counted through in order) at most 64 rows name the same one
- specialist_shares: float32 [4, 1024, 2], P(None, 'blk'), may hold values from 0.1 to 1
Outputs:
- attention_update: bfloat16 [4, 1024, 1536], P('exp', 'blk')
- expert_update: bfloat16 [4, 1024, 1536], P('exp', 'blk')
Inputs may be any that keep to these rules, and one draw needn't show every extreme that they name: `picked_specialist_labels`: the 2 ids of a hit differ. Within each event's 128 hits on one index of blk (an aligned block of 128 rows) no expert is named by more than 64 hits, a bound that some block reaches.
All inputs are finite; a program needn't handle non-finite values.
Results may differ from a plain program's by a relative error of at most 0.019.
Values may be sent and summed in bfloat16 or wider, within the bound.
A program may use at most 192 MiB of HBM per device.

v0:
```python
import math
import jax
import jax.numpy as jnp
from jax import lax
from jax.sharding import PartitionSpec as P

D = 1536
PER_LANE_DIM = 128
TOP = 2
CAP = 64


def norm_rows(values, norm_gain):
    widened = values.astype(jnp.float32)
    return (
        widened * lax.rsqrt(jnp.mean(widened * widened, axis=-1, keepdims=True) + 1e-05) * norm_gain
    )


def head_norm(values):
    return values * lax.rsqrt(jnp.mean(values * values, axis=-1, keepdims=True) + 1e-06)


def attend_hits(
    rescaled_entries,
    asking_projector,
    lookup_projector,
    content_projector,
    final_projector,
    logit_multipliers,
):
    events, row_count, model_width = rescaled_entries.shape
    common_key_heads = lookup_projector.shape[1] // PER_LANE_DIM
    local_lane_count = asking_projector.shape[1] // PER_LANE_DIM
    askers_per_lookup = local_lane_count // common_key_heads
    query_heads = jnp.einsum(
        "std,de->ste", rescaled_entries, asking_projector, preferred_element_type=jnp.float32
    )
    query_heads = head_norm(
        query_heads.reshape(events, row_count, common_key_heads, askers_per_lookup, PER_LANE_DIM)
    ).astype(jnp.bfloat16)
    key_heads = jnp.einsum(
        "std,de->ste", rescaled_entries, lookup_projector, preferred_element_type=jnp.float32
    )
    key_heads = head_norm(
        key_heads.reshape(events, row_count, common_key_heads, PER_LANE_DIM)
    ).astype(jnp.bfloat16)
    value_heads = jnp.einsum(
        "std,de->ste", rescaled_entries, content_projector, preferred_element_type=jnp.float32
    )
    value_heads = value_heads.reshape(events, row_count, common_key_heads, PER_LANE_DIM).astype(
        jnp.bfloat16
    )
    inverse_root_dim = (logit_multipliers / math.sqrt(PER_LANE_DIM)).reshape(
        common_key_heads, askers_per_lookup
    )
    key_piece = lax.all_gather(key_heads, "blk", axis=1, tiled=True)
    value_piece = lax.all_gather(value_heads, "blk", axis=1, tiled=True)
    scores = jnp.einsum(
        "sikgd,sjkd->skgij", query_heads, key_piece, preferred_element_type=jnp.float32
    )
    expo = jnp.exp(scores * inverse_root_dim[None, :, :, None, None])
    totals = jnp.sum(expo, axis=-1)
    mixture = jnp.einsum(
        "skgij,sjkd->skgid",
        expo.astype(jnp.bfloat16),
        value_piece,
        preferred_element_type=jnp.float32,
    )
    totals, mixture = (totals, mixture)
    heads_out = head_norm(mixture / totals[..., None]).astype(jnp.bfloat16)
    out_blocks = final_projector.reshape(
        common_key_heads, askers_per_lookup, PER_LANE_DIM, model_width
    )
    return jnp.einsum("skgid,kgde->sie", heads_out, out_blocks, preferred_element_type=jnp.float32)


def gates_of(labels, shares, expert_ids):
    hit = labels[..., None, :] == expert_ids[:, None]
    return jnp.sum(jnp.where(hit, shares[..., None, :], 0.0), axis=-1)


def run_experts(rows, gates, switch, widen, shrink):
    gate_act = jnp.einsum("td,jdf->tjf", rows, switch, preferred_element_type=jnp.float32)
    up_act = jnp.einsum("td,jdf->tjf", rows, widen, preferred_element_type=jnp.float32)
    hidden = (jax.nn.silu(gate_act) * up_act * gates[:, :, None]).astype(jnp.bfloat16)
    return jnp.einsum("tjf,jfd->td", hidden, shrink, preferred_element_type=jnp.float32)


def body(
    residual_deposit_sequence,
    premix_rescaler,
    asking_projector,
    lookup_projector,
    content_projector,
    final_projector,
    logit_multipliers,
    premixture_rescaler,
    specialist_switch_tensor,
    specialist_widen_tensor,
    specialist_shrink_tensor,
    picked_specialist_labels,
    specialist_shares,
):
    specialist_slot = lax.axis_index("exp")
    exp_count = lax.axis_size("exp")
    rows_all = lax.all_gather(residual_deposit_sequence, "exp", axis=0, tiled=True)
    rescaled_entries = norm_rows(rows_all, premix_rescaler).astype(jnp.bfloat16)
    local_lane_count = asking_projector.shape[1] // PER_LANE_DIM
    device_scratch = lax.dynamic_slice_in_dim(
        logit_multipliers, specialist_slot * local_lane_count, local_lane_count
    )
    partial_out = attend_hits(
        rescaled_entries,
        asking_projector,
        lookup_projector,
        content_projector,
        final_projector,
        device_scratch,
    )
    attention_full = lax.psum_scatter(
        partial_out.astype(jnp.bfloat16), "exp", scatter_dimension=0, tiled=True
    ).astype(jnp.float32)
    attention_update = attention_full.astype(jnp.bfloat16)
    residual = residual_deposit_sequence.astype(jnp.float32) + attention_full
    expert_in = norm_rows(residual, premixture_rescaler).astype(jnp.bfloat16)
    local_experts = specialist_switch_tensor.shape[0]
    expert_ids = specialist_slot * local_experts + jnp.arange(local_experts, dtype=jnp.int32)
    gates = gates_of(picked_specialist_labels, specialist_shares, expert_ids)
    rows = lax.all_gather(expert_in, "exp", axis=0, tiled=True)
    events, row_count, _ = rows.shape
    summed = run_experts(
        rows.reshape(events * row_count, D),
        gates.reshape(events * row_count, local_experts),
        specialist_switch_tensor,
        specialist_widen_tensor,
        specialist_shrink_tensor,
    ).astype(jnp.bfloat16)
    expert_update = lax.psum_scatter(
        summed.reshape(events, row_count, D), "exp", scatter_dimension=0, tiled=True
    )
    return (attention_update, expert_update)


def solution(mesh):
    placed = (
        P("exp", "blk", None),
        P(),
        P(None, "exp"),
        P(None, "exp"),
        P(None, "exp"),
        P("exp", None),
        P(),
        P(),
        P("exp", None, None),
        P("exp", None, None),
        P("exp", None, None),
        P(None, "blk", None),
        P(None, "blk", None),
    )
    return jax.shard_map(
        body,
        mesh=mesh,
        in_specs=placed,
        out_specs=(P("exp", "blk", None), P("exp", "blk", None)),
        check_vma=False,
    )
```

profile of v0, /device:TPU:0, one launch (start us, length us, event | category | flops | bytes accessed | tf_op | source)
XLA Modules:
  0.0 236.5 jit_solution(15688548943295369664)
XLA Ops:
  7.2 0.0 copy-start
  7.2 0.0 copy-start.7
  7.2 0.0 all-gather.7.cloned.1.call-start
  7.2 0.7 all-gather.7.cloned.1.call-update
  7.9 0.0 all-gather.11.cloned.1.call-start
  8.0 41.4 %all-gather.7.cloned.1.call-done = bf16[4,128,1536]{2,1,0:T(8,128)(2,1)} async-done(((bf16[1,128,1536]{2,1,0:T(8,128)(2,1)}), bf16[4,128,1536]{2,1,0:T(8,128)(2,1)}) %all-gather.7.cloned.1.call-update) | async-done | bytes 1572880 | tf_op jit(solution)/shard_map/all_gather | solution.py:107
  49.4 0.0 copy-start.2
  49.4 1.9 fusion.1
  51.3 0.0 copy-done.7
  51.3 0.0 copy-done.2
  51.4 0.0 copy-start.8
  51.4 0.0 copy-start.9
  51.4 1.5 multiply_reduce_fusion.2
  52.9 0.7 multiply_convert_fusion.6
  53.6 0.0 all-gather.11.cloned.1.call-update
  53.6 0.0 copy-start.10
  53.6 0.0 all-gather.13.cloned.1.call-start
  53.7 0.0 copy-done.8
  53.7 0.0 copy-done.9
  53.7 2.7 %convolution_convert_fusion = bf16[4,128,128]{2,1,0:T(8,128)(2,1)} fusion(bf16[4,128,1536]{2,1,0:T(8,128)(2,1)} %all-gather.7.cloned.1.call-done, f32[1536]{0:T(1024)S(1)} %copy-done.9, f32[4,128]{1,0:T(4,128)S(1)} %add_rsqrt_fusion.3, bf16[1536,128]{1,0:T(8,128)(2,1)S(1)} %copy-done.8), kind=kOutput, calls=%fused_computation.19 | convolution fusion | flops 204537856 | bytes 2105344 | tf_op jit(solution)/shard_map/std,de->ste/dot_general | solution.py:48
  56.4 0.0 all-gather.13.cloned.1.call-update
  56.4 0.0 reduce-scatter.3.cloned.1.call-start
  56.5 0.0 copy-done.10
  56.5 0.1 dynamic-slice_multiply_fusion
  56.6 3.7 %fusion.31 = (f32[4,128,384]{2,1,0:T(8,128)S(1)}, f32[4,128,384]{2,1,0:T(8,128)}) fusion(bf16[1536,384]{1,0:T(8,128)(2,1)} %param.15, bf16[4,128,1536]{2,1,0:T(8,128)(2,1)} %all-gather.7.cloned.1.call-done, f32[1536]{0:T(1024)S(1)} %copy-done.9, f32[4,128]{1,0:T(4,128)S(1)} %add_rsqrt_fusion.3), kind=kOutput, calls=%fused_computation.49 | convolution fusion | flops 607322112 | bytes 4333568 | tf_op jit(solution)/shard_map/std,de->ste/dot_general | solution.py:36
  60.2 1.2 copy.43
  61.4 1.4 copy.42
  62.8 1.2 reduce_sum.65
  64.0 12.2 %all-gather.11.cloned.1.call-done = bf16[4,1024,128]{1,2,0:T(8,128)(2,1)} async-done(((bf16[4,128,128]{1,2,0:T(8,128)(2,1)}), bf16[4,1024,128]{1,2,0:T(8,128)(2,1)}) %all-gather.11.cloned.1.call-update) | async-done | bytes 1048592 | tf_op jit(solution)/shard_map/all_gather | solution.py:57
  76.2 5.4 %bitcast_reduce_fusion = (f32[4,3,128]{2,1,0:T(4,128)S(1)}, f32[4,1024,128,3]{2,1,3,0:T(8,128)}) fusion(f32[3]{0:T(128)S(1)} %dynamic-slice_multiply_fusion, f32[4,128,3,128]{1,3,2,0:T(8,128)S(1)} %bitcast.91, f32[4,128,3]{1,2,0:T(4,128)S(1)} %add_rsqrt_fusion.1, bf16[4,1024,128]{1,2,0:T(8,128)(2,1)} %all-gather.11.cloned.1.call-done), kind=kOutput, calls=%fused_computation | convolution fusion | flops 406190592 | bytes 8138764 | tf_op jit(solution)/shard_map/sikgd,sjkd->skgij/dot_general | solution.py:59
  81.6 20.6 %all-gather.13.cloned.1.call-done = bf16[4,1024,128]{2,1,0:T(8,128)(2,1)} async-done(((bf16[4,128,128]{2,1,0:T(8,128)(2,1)}), bf16[4,1024,128]{2,1,0:T(8,128)(2,1)}) %all-gather.13.cloned.1.call-update) | async-done | bytes 1048592 | tf_op jit(solution)/shard_map/all_gather | solution.py:58
  102.2 0.0 copy-start.3
  102.2 4.4 %multiply_reduce_fusion.1 = (f32[4,3,128]{2,1,0:T(4,128)S(1)}, f32[4,3,128,128]{2,3,1,0:T(8,128)S(1)}) fusion(f32[4,3,128]{2,1,0:T(4,128)S(1)} %get-tuple-element.6, bf16[4,1024,128]{2,1,0:T(8,128)(2,1)} %all-gather.13.cloned.1.call-done, f32[4,1024,128,3]{2,1,3,0:T(8,128)} %get-tuple-element.7, f32[3]{0:T(128)S(1)} %dynamic-slice_multiply_fusion), kind=kOutput, calls=%fused_computation.31 | convolution fusion | flops 406387200 | bytes 8138764 | tf_op jit(solution)/shard_map/skgij,sjkd->skgid/dot_general | solution.py:64
  106.7 0.0 copy-done.3
  106.7 2.2 fusion.8
  108.9 0.0 copy-start.1
  108.9 0.0 copy-start.4
  108.9 0.0 reduce-scatter.3.cloned.1.call-update
  108.9 0.0 copy-start.5
  108.9 0.0 copy-start.6
  108.9 0.0 all-gather.9.cloned.1.call-start
  109.0 35.4 %reduce-scatter.3.cloned.1.call-done = bf16[1,128,1536]{2,1,0:T(8,128)(2,1)} async-done(((bf16[4,128,1536]{2,1,0:T(8,128)(2,1)}), bf16[1,128,1536]{2,1,0:T(8,128)(2,1)}) %reduce-scatter.3.cloned.1.call-update) | async-done | bytes 393232 | tf_op jit(solution)/shard_map/reduce_scatter | solution.py:121
  144.4 0.0 copy-done.1
  144.4 1.2 multiply_reduce_fusion
  145.6 0.0 copy-done.4
  145.6 1.9 multiply_convert_fusion.1
  147.5 0.0 all-gather.9.cloned.1.call-update
  147.5 0.0 reduce-scatter.5.cloned.1.call-start
  147.6 0.0 copy-done.5
  147.6 0.0 copy-done.6
  147.6 0.1 select_reduce_fusion
  147.7 36.0 %all-gather.9.cloned.1.call-done = bf16[4,128,1536]{2,1,0:T(8,128)(2,1)} async-done(((bf16[1,128,1536]{2,1,0:T(8,128)(2,1)}), bf16[4,128,1536]{2,1,0:T(8,128)(2,1)}) %all-gather.9.cloned.1.call-update) | async-done | bytes 1572880 | tf_op jit(solution)/shard_map/all_gather | solution.py:130
  183.7 4.7 %fusion.32 = f32[512,2,384]{2,0,1:T(8,128)} fusion(bf16[512,1536,1]{1,0,2:T(8,128)(2,1)} %bitcast.97, bf16[2,1536,384]{2,1,0:T(8,128)(2,1)} %param.21), kind=kOutput, calls=%fused_computation.50 | convolution fusion | flops 1207959552 | bytes 5505024 | tf_op jit(solution)/shard_map/td,jdf->tjf/dot_general | solution.py:84
  188.4 0.0 copy-done
  188.4 6.9 %fusion.9 = bf16[512,1536]{1,0:T(8,128)(2,1)} fusion(bf16[2,384,1536]{2,1,0:T(8,128)(2,1)S(1)} %copy-done, f32[512,2,384]{2,0,1:T(8,128)} %fusion.32, bf16[512,1536,1]{1,0,2:T(8,128)(2,1)} %bitcast.98, bf16[2,1536,384]{2,1,0:T(8,128)(2,1)} %param.22, f32[512,2]{0,1:T(2,128)S(1)} %bitcast.96), kind=kOutput, calls=%fused_computation.15 | convolution fusion | flops 2419458048 | bytes 9441280 | tf_op jit(solution)/shard_map/tjf,jfd->td/dot_general | solution.py:87
  195.3 0.0 reduce-scatter.5.cloned.1.call-update
  195.3 34.3 %reduce-scatter.5.cloned.1.call-done = bf16[1,128,1536]{2,1,0:T(8,128)(2,1)} async-done(((bf16[4,128,1536]{2,1,0:T(8,128)(2,1)}), bf16[1,128,1536]{2,1,0:T(8,128)(2,1)}) %reduce-scatter.5.cloned.1.call-update) | async-done | bytes 393232 | tf_op jit(solution)/shard_map/reduce_scatter | solution.py:139
  (9 shorter events, 0.1 us)
Async XLA Ops:
  7.2 181.2 %copy-start = (bf16[2,384,1536]{2,1,0:T(8,128)(2,1)S(1)}, bf16[2,384,1536]{2,1,0:T(8,128)(2,1)}, u32[]{:S(2)}) copy-start(bf16[2,384,1536]{2,1,0:T(8,128)(2,1)} %param.23) | copy-start | bytes 7077892
  7.2 44.2 %copy-start.7 = (bf16[1536,128]{1,0:T(8,128)(2,1)S(1)}, bf16[1536,128]{1,0:T(8,128)(2,1)}, u32[]{:S(2)}) copy-start(bf16[1536,128]{1,0:T(8,128)(2,1)} %param.16) | copy-start | bytes 1179652
  7.2 42.2 %all-gather.7.cloned.1.call-start = ((), (), s32[]{:S(2)}) async-start(), calls=%async_computation.2 | async-start | bytes 1966080 | tf_op jit(solution)/shard_map/all_gather | solution.py:107
  7.9 68.3 %all-gather.11.cloned.1.call-start = ((), (), s32[]{:S(2)}) async-start(), calls=%async_computation.6 | async-start | bytes 1179648 | tf_op jit(solution)/shard_map/all_gather | solution.py:57
  49.4 1.9 copy-start.2
  51.4 2.3 copy-start.8
  51.4 2.3 copy-start.9
  53.6 2.9 %copy-start.10 = (f32[12]{0:T(128)S(1)}, f32[12]{0:T(128)}, u32[]{:S(2)}) copy-start(f32[12]{0:T(128)} %param.19) | copy-start | bytes 148
  53.6 48.6 %all-gather.13.cloned.1.call-start = ((), (), s32[]{:S(2)}) async-start(), calls=%async_computation.7 | async-start | bytes 1179648 | tf_op jit(solution)/shard_map/all_gather | solution.py:58
  56.4 87.9 %reduce-scatter.3.cloned.1.call-start = ((), (), s32[]{:S(2)}) async-start(), calls=%async_computation.3 | async-start | bytes 1966080 | tf_op jit(solution)/shard_map/reduce_scatter | solution.py:121
  102.2 4.5 %copy-start.3 = (bf16[384,1536]{1,0:T(8,128)(2,1)S(1)}, bf16[384,1536]{1,0:T(8,128)(2,1)}, u32[]{:S(2)}) copy-start(bf16[384,1536]{1,0:T(8,128)(2,1)} %param.18) | copy-start | bytes 3538948
  108.9 35.5 %copy-start.1 = (bf16[1,128,1536]{2,1,0:T(8,128)(2,1)S(1)}, bf16[1,128,1536]{2,1,0:T(8,128)(2,1)}, u32[]{:S(2)}) copy-start(bf16[1,128,1536]{2,1,0:T(8,128)(2,1)} %param.13) | copy-start | bytes 1179652
  108.9 36.7 %copy-start.4 = (f32[1536]{0:T(1024)S(1)}, f32[1536]{0:T(1024)}, u32[]{:S(2)}) copy-start(f32[1536]{0:T(1024)} %param.20) | copy-start | bytes 18436
  108.9 38.6 %copy-start.5 = (s32[4,128,2]{1,2,0:T(2,128)S(1)}, s32[4,128,2]{1,2,0:T(2,128)}, u32[]{:S(2)}) copy-start(s32[4,128,2]{1,2,0:T(2,128)} %param.24) | copy-start | bytes 12292
  108.9 38.7 %copy-start.6 = (f32[4,128,2]{1,2,0:T(2,128)S(1)}, f32[4,128,2]{1,2,0:T(2,128)}, u32[]{:S(2)}) copy-start(f32[4,128,2]{1,2,0:T(2,128)} %param.25) | copy-start | bytes 12292
  108.9 74.8 %all-gather.9.cloned.1.call-start = ((), (), s32[]{:S(2)}) async-start(), calls=%async_computation.4 | async-start | bytes 1966080 | tf_op jit(solution)/shard_map/all_gather | solution.py:130
  147.5 82.1 %reduce-scatter.5.cloned.1.call-start = ((), (), s32[]{:S(2)}) async-start(), calls=%async_computation.5 | async-start | bytes 1966080 | tf_op jit(solution)/shard_map/reduce_scatter | solution.py:139
Sparse Core Ops, SparseCore 0:
  9.6 39.7 all-gather.6
  53.8 22.4 all-gather.10
  78.7 23.4 all-gather.12
  109.0 35.2 reduce-scatter.2
  147.6 36.0 all-gather.8
  195.4 34.1 reduce-scatter.4
where the time goes:
time: 237 us; the launch traced here: 236 us
  waiting for transfers between devices  181 us (76%)
  matrix products  31.5 us (13%)
  between operations  14.3 us (6%)
  other arithmetic  7.1 us (3%)
  local copies, waits for them, and re-layouts  2.62 us (1%)
    all_gather x1, waiting for transfers between devices, body(): lax.all_gather(residual_deposit_sequence, 'exp', axis=0, tiled=True)  41.4 us
    all_gather x1, waiting for transfers between devices, body(): rows = lax.all_gather(expert_in, 'exp', axis=0, tiled=True)  36 us
    reduce_scatter x1, waiting for transfers between devices, body(): lax.psum_scatter(partial_out.astype(jnp.bfloat16), 'exp', scatter_dimensi...  35.4 us
    reduce_scatter x1, waiting for transfers between devices, body(): lax.psum_scatter(summed.reshape(events, row_count, D), 'exp', scatter_dim...  34.3 us
    all_gather x1, waiting for transfers between devices, attend_hits(): value_piece = lax.all_gather(value_heads, 'blk', axis=1, tiled=True)  20.6 us
    all_gather x1, waiting for transfers between devices, attend_hits(): key_piece = lax.all_gather(key_heads, 'blk', axis=1, tiled=True)  12.2 us
    dot_general x1, matrix products, run_experts(): jnp.einsum('tjf,jfd->td', hidden, shrink, preferred_element_type=jnp.floa...  6.9 us
    dot_general x1, matrix products, attend_hits(): jnp.einsum('sikgd,sjkd->skgij', query_heads, key_piece, preferred_element...  5.4 us
  transfers between devices with their start and end apart: 6, of which 6 were waited for; matrix products, arithmetic and copies ran while one was open for 7% of the time, Pallas kernels for 0%

commit v1 on v0

--- a/solution.py
+++ b/solution.py
@@ -54,7 +54,13 @@
     inverse_root_dim = (logit_multipliers / math.sqrt(PER_LANE_DIM)).reshape(
         common_key_heads, askers_per_lookup
     )
-    key_piece = lax.all_gather(key_heads, "blk", axis=1, tiled=True)
+    size = lax.axis_size("blk")
+    held, blocks = (key_heads, [key_heads])
+    for _ in range(size - 1):
+        held = lax.ppermute(held, "blk", [(i, (i + 1) % size) for i in range(size)])
+        blocks.insert(0, held)
+    line = jnp.concatenate(blocks, axis=1)
+    key_piece = jnp.roll(line, (lax.axis_index("blk") + 1) * key_heads.shape[1], axis=1)
     value_piece = lax.all_gather(value_heads, "blk", axis=1, tiled=True)
     scores = jnp.einsum(
         "sikgd,sjkd->skgij", query_heads, key_piece, preferred_element_type=jnp.float32

time: 237 us -> 237 us (level)
  local copies, waits for them, and re-layouts: 2.62 us -> 9.25 us
  waiting for transfers between devices: 181 us -> 175 us
    ppermute x0 -> x7, waiting for transfers between devices: none -> 29.1 us  [attend_hits(): held = lax.ppermute(held, 'blk', [(i, (i + 1) % size) for i in range(size)])]
    all_gather x1, waiting for transfers between devices: 20.6 us -> 0.01 us  [attend_hits(): value_piece = lax.all_gather(value_heads, 'blk', axis=1, tiled=True)]
    all_gather x1 -> x0, waiting for transfers between devices: 12.2 us -> none  [attend_hits(): key_piece = lax.all_gather(key_heads, 'blk', axis=1, tiled=True)]
    unnamed x25 -> x45, local copies, waits for them, and re-layouts: 0.07 us -> 6.69 us
  transfers between devices with their start and end apart: 6 -> 12, of which waited for: 6 -> 10; matrix products, arithmetic and copies ran while one was open for 7% -> 9% of each run, Pallas kernels for 0% -> 0%
where the time goes in v1:
time: 237 us; the launch traced here: 236 us
  waiting for transfers between devices  175 us (74%)
  matrix products  30.5 us (13%)
  between operations  14.1 us (6%)
  local copies, waits for them, and re-layouts  9.25 us (4%)
  other arithmetic  6.76 us (3%)
    all_gather x1, waiting for transfers between devices, body(): lax.all_gather(residual_deposit_sequence, 'exp', axis=0, tiled=True)  41.4 us
    all_gather x1, waiting for transfers between devices, body(): rows = lax.all_gather(expert_in, 'exp', axis=0, tiled=True)  36 us
    reduce_scatter x1, waiting for transfers between devices, body(): lax.psum_scatter(summed.reshape(events, row_count, D), 'exp', scatter_dim...  34.3 us
    reduce_scatter x1, waiting for transfers between devices, body(): lax.psum_scatter(partial_out.astype(jnp.bfloat16), 'exp', scatter_dimensi...  33.4 us
    ppermute x7, waiting for transfers between devices, attend_hits(): held = lax.ppermute(held, 'blk', [(i, (i + 1) % size) for i in range(size)])  29.1 us
    dot_general x1, matrix products, run_experts(): jnp.einsum('tjf,jfd->td', hidden, shrink, preferred_element_type=jnp.floa...  6.91 us
    unnamed x45, local copies, waits for them, and re-layouts  6.69 us
  transfers between devices with their start and end apart: 12, of which 10 were waited for; matrix products, arithmetic and copies ran while one was open for 9% of the time, Pallas kernels for 0%

profile of v1, /device:TPU:0, one launch (start us, length us, event | category | flops | bytes accessed | tf_op | source)
XLA Modules:
  0.0 236.0 jit_solution(346614107656178426)
XLA Ops:
  7.2 0.0 copy-start
  7.2 0.0 all-gather.5.cloned.1.call-start
  7.2 0.7 all-gather.5.cloned.1.call-update
  7.9 0.0 all-gather.9.cloned.1.call-start
  8.0 41.4 %all-gather.5.cloned.1.call-done = bf16[4,128,1536]{2,1,0:T(8,128)(2,1)} async-done(((bf16[1,128,1536]{2,1,0:T(8,128)(2,1)}), bf16[4,128,1536]{2,1,0:T(8,128)(2,1)}) %all-gather.5.cloned.1.call-update) | async-done | bytes 1572880 | tf_op jit(solution)/shard_map/all_gather | solution.py:113
  49.4 1.8 fusion.1
  51.2 0.0 copy-start.12
  51.2 2.2 multiply_reduce_fusion.2
  53.5 0.1 fusion.26
  53.6 0.1 collective-permute-start
  53.7 5.3 %collective-permute-done = bf16[4,128,1,128]{3,1,0,2:T(8,128)(2,1)S(1)} collective-permute-done((bf16[4,128,1,128]{3,1,0,2:T(8,128)(2,1)S(1)}, bf16[4,128,1,128]{3,1,0,2:T(8,128)(2,1)S(1)}, u32[]{:S(2)}, u32[]{:S(2)}) %collective-permute-start) | collective-permute-done | bytes 131104 | tf_op jit(solution)/shard_map/ppermute | solution.py:60
  59.0 0.0 collective-permute-start.1
  59.0 5.3 %collective-permute-done.1 = bf16[4,128,1,128]{3,1,0,2:T(8,128)(2,1)S(1)} collective-permute-done((bf16[4,128,1,128]{3,1,0,2:T(8,128)(2,1)S(1)}, bf16[4,128,1,128]{3,1,0,2:T(8,128)(2,1)S(1)}, u32[]{:S(2)}, u32[]{:S(2)}) %collective-permute-start.1) | collective-permute-done | bytes 131104 | tf_op jit(solution)/shard_map/ppermute | solution.py:60
  64.3 0.0 collective-permute-start.2
  64.3 5.3 %collective-permute-done.2 = bf16[4,128,1,128]{3,1,0,2:T(8,128)(2,1)S(1)} collective-permute-done((bf16[4,128,1,128]{3,1,0,2:T(8,128)(2,1)S(1)}, bf16[4,128,1,128]{3,1,0,2:T(8,128)(2,1)S(1)}, u32[]{:S(2)}, u32[]{:S(2)}) %collective-permute-start.2) | collective-permute-done | bytes 131104 | tf_op jit(solution)/shard_map/ppermute | solution.py:60
  69.6 0.0 collective-permute-start.3
  69.6 0.0 copy-done.13
  69.6 0.1 dynamic-slice_multiply_fusion
  69.7 5.2 %collective-permute-done.3 = bf16[4,128,1,128]{3,1,0,2:T(8,128)(2,1)S(1)} collective-permute-done((bf16[4,128,1,128]{3,1,0,2:T(8,128)(2,1)S(1)}, bf16[4,128,1,128]{3,1,0,2:T(8,128)(2,1)S(1)}, u32[]{:S(2)}, u32[]{:S(2)}) %collective-permute-start.3) | collective-permute-done | bytes 131104 | tf_op jit(solution)/shard_map/ppermute | solution.py:60
  74.9 0.0 collective-permute-start.4
  74.9 0.0 copy-done.12
  74.9 2.7 %convolution_convert_fusion = bf16[4,128,128]{2,1,0:T(8,128)(2,1)} fusion(bf16[4,128,1536]{2,1,0:T(8,128)(2,1)} %all-gather.5.cloned.1.call-done, f32[1536]{0:T(1024)} %param.14, f32[4,128]{1,0:T(4,128)S(1)} %add_rsqrt_fusion.3, bf16[1536,128]{1,0:T(8,128)(2,1)S(1)} %copy-done.12), kind=kOutput, calls=%fused_computation.19 | convolution fusion | flops 204537856 | bytes 2105344 | tf_op jit(solution)/shard_map/std,de->ste/dot_general | solution.py:48
  77.6 0.0 all-gather.9.cloned.1.call-update
  77.6 0.0 reduce-scatter.3.cloned.1.call-start
  77.7 2.6 %collective-permute-done.4 = bf16[4,128,1,128]{3,1,0,2:T(8,128)(2,1)} collective-permute-done((bf16[4,128,1,128]{3,1,0,2:T(8,128)(2,1)S(1)}, bf16[4,128,1,128]{3,1,0,2:T(8,128)(2,1)}, u32[]{:S(2)}, u32[]{:S(2)}) %collective-permute-start.4) | collective-permute-done | bytes 131104 | tf_op jit(solution)/shard_map/ppermute | solution.py:60
  80.3 0.0 copy-done.4
  80.3 0.1 collective-permute-start.5
  80.3 3.7 %fusion.29 = (f32[4,128,384]{2,1,0:T(8,128)S(1)}, f32[4,128,384]{2,1,0:T(8,128)}) fusion(bf16[1536,384]{1,0:T(8,128)(2,1)} %param.15, bf16[4,128,1536]{2,1,0:T(8,128)(2,1)} %all-gather.5.cloned.1.call-done, f32[1536]{0:T(1024)} %param.14, f32[4,128]{1,0:T(4,128)S(1)} %add_rsqrt_fusion.3), kind=kOutput, calls=%fused_computation.68 | convolution fusion | flops 607322112 | bytes 4333568 | tf_op jit(solution)/shard_map/std,de->ste/dot_general | solution.py:36
  84.0 1.2 copy.36
  85.2 1.4 copy.35
  86.6 1.2 reduce_sum.65
  87.8 0.0 copy-start.7
  87.8 0.0 copy-start.5
  87.8 0.0 collective-permute-done.5
  87.8 0.1 collective-permute-start.6
  87.9 5.5 %collective-permute-done.6 = bf16[4,128,1,128]{3,1,0,2:T(8,128)(2,1)S(1)} collective-permute-done((bf16[4,128,1,128]{3,1,0,2:T(8,128)(2,1)}, bf16[4,128,1,128]{3,1,0,2:T(8,128)(2,1)S(1)}, u32[]{:S(2)}, u32[]{:S(2)}) %collective-permute-start.6) | collective-permute-done | bytes 131104 | tf_op jit(solution)/shard_map/ppermute | solution.py:60
  93.4 0.9 constant_dynamic-update-slice_fusion.14
  94.3 0.9 constant_dynamic-update-slice_fusion.13
  95.2 0.9 constant_dynamic-update-slice_fusion.12
  96.2 0.9 constant_dynamic-update-slice_fusion.11
  97.1 0.9 constant_dynamic-update-slice_fusion.10
  98.0 0.2 constant_dynamic-update-slice_fusion.8
  98.2 0.9 constant_dynamic-update-slice_fusion.6
  99.2 0.9 constant_dynamic-update-slice_fusion.5
  100.2 0.0 copy-done.3
  100.2 0.2 constant_dynamic-update-slice_fusion
  100.4 3.7 %bitcast_reduce_fusion = (f32[4,3,128]{2,1,0:T(4,128)S(1)}, f32[4,1024,128,3]{2,1,3,0:T(8,128)}) fusion(f32[3]{0:T(128)S(1)} %dynamic-slice_multiply_fusion, f32[4,128,3,128]{1,3,2,0:T(8,128)S(1)} %bitcast.90, f32[4,128,3]{1,2,0:T(4,128)S(1)} %add_rsqrt_fusion.1, bf16[4,2048,1,128]{3,1,0,2:T(8,128)(2,1)S(1)} %constant_dynamic-update-slice_fusion, s32[]{:T(128)S(6)} %select_n.21), kind=kOutput, calls=%fused_computation | convolution fusion | flops 406190592 | bytes 8141316 | tf_op jit(solution)/shard_map/sikgd,sjkd->skgij/dot_general | solution.py:65
  104.1 4.4 %multiply_reduce_fusion.1 = (f32[4,3,128]{2,1,0:T(4,128)S(1)}, f32[4,3,128,128]{2,3,1,0:T(8,128)S(1)}) fusion(f32[4,3,128]{2,1,0:T(4,128)S(1)} %get-tuple-element.6, bf16[4,1024,128]{2,1,0:T(8,128)(2,1)} %all-gather.9.cloned.1.call-done, f32[4,1024,128,3]{2,1,3,0:T(8,128)} %get-tuple-element.7, f32[3]{0:T(128)S(1)} %dynamic-slice_multiply_fusion), kind=kOutput, calls=%fused_computation.31 | convolution fusion | flops 406387200 | bytes 8138764 | tf_op jit(solution)/shard_map/skgij,sjkd->skgid/dot_general | solution.py:70
  108.5 0.0 copy-start.1
  108.5 2.2 fusion.8
  110.7 0.0 reduce-scatter.3.cloned.1.call-update
  110.8 0.0 all-gather.7.cloned.1.call-start
  110.8 33.4 %reduce-scatter.3.cloned.1.call-done = bf16[1,128,1536]{2,1,0:T(8,128)(2,1)} async-done(((bf16[4,128,1536]{2,1,0:T(8,128)(2,1)}), bf16[1,128,1536]{2,1,0:T(8,128)(2,1)}) %reduce-scatter.3.cloned.1.call-update) | async-done | bytes 393232 | tf_op jit(solution)/shard_map/reduce_scatter | solution.py:127
  144.2 1.2 multiply_reduce_fusion
  145.4 0.0 copy-done.8
  145.4 1.9 multiply_convert_fusion.1
  147.3 0.0 all-gather.7.cloned.1.call-update
  147.3 0.0 reduce-scatter.5.cloned.1.call-start
  147.4 0.1 select_reduce_fusion
  147.5 36.0 %all-gather.7.cloned.1.call-done = bf16[4,128,1536]{2,1,0:T(8,128)(2,1)} async-done(((bf16[1,128,1536]{2,1,0:T(8,128)(2,1)}), bf16[4,128,1536]{2,1,0:T(8,128)(2,1)}) %all-gather.7.cloned.1.call-update) | async-done | bytes 1572880 | tf_op jit(solution)/shard_map/all_gather | solution.py:136
  183.6 4.7 %fusion.30 = f32[512,2,384]{2,0,1:T(8,128)} fusion(bf16[512,1536,1]{1,0,2:T(8,128)(2,1)} %bitcast.95, bf16[2,1536,384]{2,1,0:T(8,128)(2,1)} %param.21), kind=kOutput, calls=%fused_computation.69 | convolution fusion | flops 1207959552 | bytes 5505024 | tf_op jit(solution)/shard_map/td,jdf->tjf/dot_general | solution.py:90
  188.2 6.9 %fusion.9 = bf16[512,1536]{1,0:T(8,128)(2,1)} fusion(bf16[2,384,1536]{2,1,0:T(8,128)(2,1)S(1)} %copy-done, f32[512,2,384]{2,0,1:T(8,128)} %fusion.30, bf16[512,1536,1]{1,0,2:T(8,128)(2,1)} %bitcast.96, bf16[2,1536,384]{2,1,0:T(8,128)(2,1)} %param.22, f32[512,2]{0,1:T(2,128)S(1)} %bitcast.94), kind=kOutput, calls=%fused_computation.15 | convolution fusion | flops 2419458048 | bytes 9441280 | tf_op jit(solution)/shard_map/tjf,jfd->td/dot_general | solution.py:93
  195.1 0.0 reduce-scatter.5.cloned.1.call-update
  195.2 34.3 %reduce-scatter.5.cloned.1.call-done = bf16[1,128,1536]{2,1,0:T(8,128)(2,1)} async-done(((bf16[4,128,1536]{2,1,0:T(8,128)(2,1)}), bf16[1,128,1536]{2,1,0:T(8,128)(2,1)}) %reduce-scatter.5.cloned.1.call-update) | async-done | bytes 393232 | tf_op jit(solution)/shard_map/reduce_scatter | solution.py:145
  (35 shorter events, 0.2 us)
Async XLA Ops:
  7.2 181.1 %copy-start = (bf16[2,384,1536]{2,1,0:T(8,128)(2,1)S(1)}, bf16[2,384,1536]{2,1,0:T(8,128)(2,1)}, u32[]{:S(2)}) copy-start(bf16[2,384,1536]{2,1,0:T(8,128)(2,1)} %param.23) | copy-start | bytes 7077892
  7.2 42.2 %all-gather.5.cloned.1.call-start = ((), (), s32[]{:S(2)}) async-start(), calls=%async_computation.2 | async-start | bytes 1966080 | tf_op jit(solution)/shard_map/all_gather | solution.py:113
  7.9 96.2 %all-gather.9.cloned.1.call-start = ((), (), s32[]{:S(2)}) async-start(), calls=%async_computation.6 | async-start | bytes 1179648 | tf_op jit(solution)/shard_map/all_gather | solution.py:64
  51.2 18.4 %copy-start.13 = (f32[12]{0:T(128)S(1)}, f32[12]{0:T(128)}, u32[]{:S(2)}) copy-start(f32[12]{0:T(128)} %param.19) | copy-start | bytes 148
  51.2 23.7 %copy-start.12 = (bf16[1536,128]{1,0:T(8,128)(2,1)S(1)}, bf16[1536,128]{1,0:T(8,128)(2,1)}, u32[]{:S(2)}) copy-start(bf16[1536,128]{1,0:T(8,128)(2,1)} %param.17) | copy-start | bytes 1179652
  53.6 5.3 %collective-permute-start = (bf16[4,128,1,128]{3,1,0,2:T(8,128)(2,1)S(1)}, bf16[4,128,1,128]{3,1,0,2:T(8,128)(2,1)S(1)}, u32[]{:S(2)}, u32[]{:S(2)}) collective-permute-start(bf16[4,128,1,128]{3,1,0,2:T(8,128)(2,1)S(1)} %fusion.26), channel_id=1, source_target_pairs={{0,4},{4,8},{8,12},{12,16},{16,20},{20,24},{24,28},{28,0},{1,5},{5... | collective-permute-start | bytes 393224 | tf_op jit(solution)/shard_map/ppermute | solution.py:60
  59.0 5.3 %collective-permute-start.1 = (bf16[4,128,1,128]{3,1,0,2:T(8,128)(2,1)S(1)}, bf16[4,128,1,128]{3,1,0,2:T(8,128)(2,1)S(1)}, u32[]{:S(2)}, u32[]{:S(2)}) collective-permute-start(bf16[4,128,1,128]{3,1,0,2:T(8,128)(2,1)S(1)} %collective-permute-done), channel_id=1, source_target_pairs={{0,4},{4,8},{8,12},{12,16},{16,20},{20,24},{24,28},{28,0},{1,5},{5... | collective-permute-start | bytes 393224 | tf_op jit(solution)/shard_map/ppermute | solution.py:60
  64.3 16.0 %copy-start.2 = (bf16[4,128,1,128]{3,1,0,2:T(8,128)(2,1)}, bf16[4,128,1,128]{3,1,0,2:T(8,128)(2,1)S(1)}, u32[]{:S(2)}) copy-start(bf16[4,128,1,128]{3,1,0,2:T(8,128)(2,1)S(1)} %collective-permute-done.1) | copy-start | bytes 393220
  64.3 5.3 %collective-permute-start.2 = (bf16[4,128,1,128]{3,1,0,2:T(8,128)(2,1)S(1)}, bf16[4,128,1,128]{3,1,0,2:T(8,128)(2,1)S(1)}, u32[]{:S(2)}, u32[]{:S(2)}) collective-permute-start(bf16[4,128,1,128]{3,1,0,2:T(8,128)(2,1)S(1)} %collective-permute-done.1), channel_id=1, source_target_pairs={{0,4},{4,8},{8,12},{12,16},{16,20},{20,24},{24,28},{28,0},{1,5},{5... | collective-permute-start | bytes 393224 | tf_op jit(solution)/shard_map/ppermute | solution.py:60
  69.6 10.7 %copy-start.4 = (bf16[4,128,1,128]{3,1,0,2:T(8,128)(2,1)}, bf16[4,128,1,128]{3,1,0,2:T(8,128)(2,1)S(1)}, u32[]{:S(2)}) copy-start(bf16[4,128,1,128]{3,1,0,2:T(8,128)(2,1)S(1)} %collective-permute-done.2) | copy-start | bytes 393220
  69.6 5.3 %collective-permute-start.3 = (bf16[4,128,1,128]{3,1,0,2:T(8,128)(2,1)S(1)}, bf16[4,128,1,128]{3,1,0,2:T(8,128)(2,1)S(1)}, u32[]{:S(2)}, u32[]{:S(2)}) collective-permute-start(bf16[4,128,1,128]{3,1,0,2:T(8,128)(2,1)S(1)} %collective-permute-done.2), channel_id=1, source_target_pairs={{0,4},{4,8},{8,12},{12,16},{16,20},{20,24},{24,28},{28,0},{1,5},{5... | collective-permute-start | bytes 393224 | tf_op jit(solution)/shard_map/ppermute | solution.py:60
  74.9 5.4 %copy-start.6 = (bf16[4,128,1,128]{3,1,0,2:T(8,128)(2,1)}, bf16[4,128,1,128]{3,1,0,2:T(8,128)(2,1)S(1)}, u32[]{:S(2)}) copy-start(bf16[4,128,1,128]{3,1,0,2:T(8,128)(2,1)S(1)} %collective-permute-done.3) | copy-start | bytes 393220
  74.9 5.4 %collective-permute-start.4 = (bf16[4,128,1,128]{3,1,0,2:T(8,128)(2,1)S(1)}, bf16[4,128,1,128]{3,1,0,2:T(8,128)(2,1)}, u32[]{:S(2)}, u32[]{:S(2)}) collective-permute-start(bf16[4,128,1,128]{3,1,0,2:T(8,128)(2,1)S(1)} %collective-permute-done.3), channel_id=1, source_target_pairs={{0,4},{4,8},{8,12},{12,16},{16,20},{20,24},{24,28},{28,0},{1,5},{5... | collective-permute-start | bytes 393224 | tf_op jit(solution)/shard_map/ppermute | solution.py:60
  77.6 66.5 %reduce-scatter.3.cloned.1.call-start = ((), (), s32[]{:S(2)}) async-start(), calls=%async_computation.3 | async-start | bytes 1966080 | tf_op jit(solution)/shard_map/reduce_scatter | solution.py:127
  80.3 7.5 %collective-permute-start.5 = (bf16[4,128,1,128]{3,1,0,2:T(8,128)(2,1)}, bf16[4,128,1,128]{3,1,0,2:T(8,128)(2,1)}, u32[]{:S(2)}, u32[]{:S(2)}) collective-permute-start(bf16[4,128,1,128]{3,1,0,2:T(8,128)(2,1)} %collective-permute-done.4), channel_id=1, source_target_pairs={{0,4},{4,8},{8,12},{12,16},{16,20},{20,24},{24,28},{28,0},{1,5},{5... | collective-permute-start | bytes 393224 | tf_op jit(solution)/shard_map/ppermute | solution.py:60
  87.8 12.3 %copy-start.7 = (bf16[4,128,1,128]{3,1,0,2:T(8,128)(2,1)S(1)}, bf16[4,128,1,128]{3,1,0,2:T(8,128)(2,1)}, u32[]{:S(2)}) copy-start(bf16[4,128,1,128]{3,1,0,2:T(8,128)(2,1)} %copy-done.6) | copy-start | bytes 393220
  87.8 12.4 %copy-start.5 = (bf16[4,128,1,128]{3,1,0,2:T(8,128)(2,1)S(1)}, bf16[4,128,1,128]{3,1,0,2:T(8,128)(2,1)}, u32[]{:S(2)}) copy-start(bf16[4,128,1,128]{3,1,0,2:T(8,128)(2,1)} %copy-done.4) | copy-start | bytes 393220
  87.8 12.4 %copy-start.3 = (bf16[4,128,1,128]{3,1,0,2:T(8,128)(2,1)S(1)}, bf16[4,128,1,128]{3,1,0,2:T(8,128)(2,1)}, u32[]{:S(2)}) copy-start(bf16[4,128,1,128]{3,1,0,2:T(8,128)(2,1)} %copy-done.2) | copy-start | bytes 393220
  87.8 5.6 %collective-permute-start.6 = (bf16[4,128,1,128]{3,1,0,2:T(8,128)(2,1)}, bf16[4,128,1,128]{3,1,0,2:T(8,128)(2,1)S(1)}, u32[]{:S(2)}, u32[]{:S(2)}) collective-permute-start(bf16[4,128,1,128]{3,1,0,2:T(8,128)(2,1)} %collective-permute-done.5), channel_id=1, source_target_pairs={{0,4},{4,8},{8,12},{12,16},{16,20},{20,24},{24,28},{28,0},{1,5},{5... | collective-permute-start | bytes 393224 | tf_op jit(solution)/shard_map/ppermute | solution.py:60
  104.1 4.5 %copy-start.11 = (bf16[384,1536]{1,0:T(8,128)(2,1)S(1)}, bf16[384,1536]{1,0:T(8,128)(2,1)}, u32[]{:S(2)}) copy-start(bf16[384,1536]{1,0:T(8,128)(2,1)} %param.18) | copy-start | bytes 3538948
  108.5 35.7 %copy-start.1 = (bf16[1,128,1536]{2,1,0:T(8,128)(2,1)S(1)}, bf16[1,128,1536]{2,1,0:T(8,128)(2,1)}, u32[]{:S(2)}) copy-start(bf16[1,128,1536]{2,1,0:T(8,128)(2,1)} %param.13) | copy-start | bytes 1179652
  110.7 34.7 %copy-start.8 = (f32[1536]{0:T(1024)S(1)}, f32[1536]{0:T(1024)}, u32[]{:S(2)}) copy-start(f32[1536]{0:T(1024)} %param.20) | copy-start | bytes 18436
  110.7 36.7 %copy-start.9 = (s32[4,128,2]{1,2,0:T(2,128)S(1)}, s32[4,128,2]{1,2,0:T(2,128)}, u32[]{:S(2)}) copy-start(s32[4,128,2]{1,2,0:T(2,128)} %param.24) | copy-start | bytes 12292
  110.7 36.7 %copy-start.10 = (f32[4,128,2]{1,2,0:T(2,128)S(1)}, f32[4,128,2]{1,2,0:T(2,128)}, u32[]{:S(2)}) copy-start(f32[4,128,2]{1,2,0:T(2,128)} %param.25) | copy-start | bytes 12292
  110.8 72.8 %all-gather.7.cloned.1.call-start = ((), (), s32[]{:S(2)}) async-start(), calls=%async_computation.4 | async-start | bytes 1966080 | tf_op jit(solution)/shard_map/all_gather | solution.py:136
  147.3 82.2 %reduce-scatter.5.cloned.1.call-start = ((), (), s32[]{:S(2)}) async-start(), calls=%async_computation.5 | async-start | bytes 1966080 | tf_op jit(solution)/shard_map/reduce_scatter | solution.py:145
Sparse Core Ops, SparseCore 0:
  9.6 39.7 all-gather.4
  77.8 22.9 all-gather.8
  110.9 33.2 reduce-scatter.2
  147.4 36.0 all-gather.6
  195.3 34.1 reduce-scatter.4
